TPU v7x, 512 devices: a whole 4x8x8 slice. The times are simulated.
512 devices in a mesh: snap: 8 (over z), tile: 64 (over x, y, core).
Axes of the slice: x: 4, y: 8, z: 8, core: 2. Of those that a mesh axis runs over, the one named last changes fastest.
Arguments:
- modes: bfloat16 [8192, 256], P(('snap', 'tile')), may hold values from -8 to 8
- targets: bfloat16 [8192, 256], P(('snap', 'tile')), may hold values from -16 to 16
- pairs: int32 [4096, 2], replicated, may hold values from 0 to 256, as said below
- support: int32 [4096, 256], P(('snap', 'tile')), may hold values from 0 to 1, as said below
Outputs:
- coeffs: float32 [4096, 256], P(('snap', 'tile'))
- resid: float32 [4096, 256], P(('snap', 'tile'))
Inputs may be any that keep to these rules, and one draw needn't show every extreme that they name: Rows are distinct unordered pairs; the first entry is below 256; every index below 256 is the first entry of exactly 16 rows. `support`: every target has at least one active term.
All inputs are finite; a program needn't handle non-finite values.
Results may differ from a plain program's by a relative error of at most 0.0036.
Values may be sent and summed in bfloat16 or wider, within the bound.
A program may use at most 64 MiB of HBM per device.

v0:
```python
import jax
import jax.numpy as jnp
from jax import lax
from jax.sharding import PartitionSpec as P

ITERS = 2


def widened(rows_in):
    return jnp.concatenate(
        [rows_in.astype(jnp.float32), jnp.ones((rows_in.shape[0], 1), jnp.float32)], axis=1
    )


def body(modes, targets, pairs, support):
    snap_count = lax.axis_size("snap")
    tile_count = lax.axis_size("tile")
    term_count = pairs.shape[0]
    mode_count = modes.shape[1]
    target_count = targets.shape[1]
    share_rows = term_count // (snap_count * tile_count)
    total_snaps = modes.shape[0] * snap_count * tile_count
    tile_at = lax.axis_index("tile")
    term_grid = jnp.arange(term_count, dtype=jnp.int32).reshape(snap_count, tile_count, share_rows)
    own_terms = lax.dynamic_index_in_dim(term_grid, tile_at, 1, keepdims=False).reshape(-1)
    first_factor = pairs[:, 0]
    second_factor = pairs[:, 1]
    start_sums = (
        jnp.zeros((snap_count * share_rows, term_count), jnp.float32),
        jnp.zeros((snap_count * share_rows, target_count), jnp.float32),
    )
    rows_in = lax.all_gather(modes, "tile", axis=0, tiled=True)
    count_rows = rows_in.shape[0]
    block_rows = max((divisor for divisor in range(1, 513) if count_rows % divisor == 0))

    def inner(totals, block_item):
        block_modes, block_targets = block_item
        extended = widened(block_modes)
        library = (
            jnp.take(extended, first_factor, axis=1) * jnp.take(extended, second_factor, axis=1)
        ).astype(jnp.bfloat16)
        mine = jnp.take(library, own_terms, axis=1)
        gram_sum = totals[0] + lax.dot_general(
            mine, library, (((0,), (0,)), ((), ())), preferred_element_type=jnp.float32
        )
        cross_sum = totals[1] + lax.dot_general(
            mine, block_targets, (((0,), (0,)), ((), ())), preferred_element_type=jnp.float32
        )
        return ((gram_sum, cross_sum), None)

    blocks = (
        rows_in.reshape(count_rows // block_rows, block_rows, mode_count),
        lax.all_gather(targets, "tile", axis=0, tiled=True).reshape(
            count_rows // block_rows, block_rows, target_count
        ),
    )
    results, _ = lax.scan(inner, start_sums, blocks)
    gram_part, cross_part = results
    gram_all, cross_all = lax.psum((gram_part, cross_part), "snap")
    snap_at = lax.axis_index("snap")
    gram_rows = lax.dynamic_slice_in_dim(gram_all, snap_at * share_rows, share_rows, 0)
    cross_rows = lax.dynamic_slice_in_dim(cross_all, snap_at * share_rows, share_rows, 0)
    gram_rows = gram_rows / total_snaps
    cross_rows = cross_rows / total_snaps
    support_mask = support.astype(jnp.float32)

    def energy_of(vector):
        return lax.psum(jnp.sum(vector * vector, axis=0), ("snap", "tile"))

    resid = support_mask * cross_rows
    coeffs = jnp.zeros_like(resid)
    direction = resid
    energy = energy_of(resid)
    for step in range(ITERS):
        product = jnp.dot(
            gram_rows,
            lax.all_gather(direction, ("snap", "tile"), axis=0, tiled=True),
            precision=lax.Precision.HIGHEST,
            preferred_element_type=jnp.float32,
        )
        image = support_mask * product
        step_len = energy / lax.psum(jnp.sum(direction * image, axis=0), ("snap", "tile"))
        coeffs = coeffs + step_len * direction
        resid = resid - step_len * image
        if step + 1 < ITERS:
            fresh = energy_of(resid)
            direction = resid + fresh / energy * direction
            energy = fresh
    return (coeffs, resid)


def solution(mesh):
    return jax.shard_map(
        body,
        mesh=mesh,
        in_specs=(
            P(("snap", "tile"), None),
            P(("snap", "tile"), None),
            P(),
            P(("snap", "tile"), None),
        ),
        out_specs=(P(("snap", "tile"), None), P(("snap", "tile"), None)),
        check_vma=False,
    )
```

profile of v0, /device:TPU:1, one launch (start us, length us, event | category | flops | bytes accessed | tf_op | source)
XLA Modules:
  0.0 834.8 jit_solution(8397565621540414149)
XLA Ops:
  7.2 0.0 all-reduce.5.cloned.1.call-start
  7.2 0.1 reshape.63
  7.3 0.9 fusion.16
  8.2 54.4 %all_gather.12 = bf16[1024,256]{1,0:T(8,128)(2,1)S(1)} all-gather(bf16[16,256]{1,0:T(8,128)(2,1)} %param.8), channel_id=1, replica_groups=mesh['snap'=8,'tile'=64] {'tile'}, dimensions={0}, use_global_device_ids=true | all-gather | bytes 532480 | tf_op jit(solution)/shard_map/all_gather | solution.py:32
  62.6 49.5 %all_gather.13 = bf16[1024,256]{1,0:T(8,128)(2,1)S(1)} all-gather(bf16[16,256]{1,0:T(8,128)(2,1)} %param.9), channel_id=1, replica_groups=mesh['snap'=8,'tile'=64] {'tile'}, dimensions={0}, use_global_device_ids=true | all-gather | bytes 532480 | tf_op jit(solution)/shard_map/all_gather | solution.py:53
  112.0 0.0 copy-start.4
  112.0 101.3 %while.13 = (s32[]{:T(128)}, f32[64,4096]{1,0:T(8,128)S(1)}, f32[64,256]{1,0:T(8,128)S(1)}, s32[64]{0:T(128)S(1)}, bf16[2,512,256]{2,1,0:T(8,128)(2,1)S(1)}, /*i...) while((s32[]{:T(128)}, f32[64,4096]{1,0:T(8,128)S(1)}, ...), condition=%wide.region_1.3_spmd.clone, body=%wide.region_0.2_spmd.clone.sunk | while | flops 294438976 | bytes 63463412 | solution.py:57
  112.1 0.1 copy.9
  112.2 0.1 pad_convert_fusion.2
  112.3 16.9 %gather_fusion.1 = f32[4096,512]{1,0:T(8,128)} fusion(f32[512,257]{0,1:T(8,128)S(1)} %pad_convert_fusion.2, s32[4096]{0:T(1024)S(1)} %get-tuple-element.170), kind=kCustom, calls=%fused_computation.clone.clone.1 | custom fusion | bytes 16793600 | tf_op jit(solution)/shard_map/while/body/eval_jaxpr/jit(_take)/gather | solution.py:40
  129.2 16.9 %gather_fusion = f32[4096,512]{1,0:T(8,128)} fusion(f32[512,257]{0,1:T(8,128)S(1)} %pad_convert_fusion.2, s32[4096]{0:T(1024)S(1)} %get-tuple-element.169), kind=kCustom, calls=%fused_computation.1.clone.clone.1 | custom fusion | bytes 16793600 | tf_op jit(solution)/shard_map/while/body/eval_jaxpr/jit(_take)/gather | solution.py:40
  146.1 9.2 %fusion.28 = bf16[512,4096]{0,1:T(8,128)(2,1)} fusion(f32[4096,512]{1,0:T(8,128)} %gather_fusion, f32[4096,512]{1,0:T(8,128)} %gather_fusion.1, pred[4096]{0:T(1024)(128)(4,1)S(1)} %get-tuple-element.171, pred[4096]{0:T(1024)(128)(4,1)S(1)} %get-tuple-element.172), kind=kLoop, calls=%fused_computation.4.clone.1 | loop fusion | flops 8388608 | bytes 20979712 | tf_op jit(solution)/shard_map/while/body/eval_jaxpr/convert_element_type | solution.py:41
  155.3 3.4 gather_fusion.2
  158.8 3.7 convolution_add_fusion.4
  162.4 0.2 convolution_add_fusion.5
  162.7 0.1 copy.9
  162.9 0.1 pad_convert_fusion.2
  163.0 16.9 %gather_fusion.1 = f32[4096,512]{1,0:T(8,128)} fusion(f32[512,257]{0,1:T(8,128)S(1)} %pad_convert_fusion.2, s32[4096]{0:T(1024)S(1)} %get-tuple-element.170), kind=kCustom, calls=%fused_computation.clone.clone.1 | custom fusion | bytes 16793600 | tf_op jit(solution)/shard_map/while/body/eval_jaxpr/jit(_take)/gather | solution.py:40
  179.8 16.9 %gather_fusion = f32[4096,512]{1,0:T(8,128)} fusion(f32[512,257]{0,1:T(8,128)S(1)} %pad_convert_fusion.2, s32[4096]{0:T(1024)S(1)} %get-tuple-element.169), kind=kCustom, calls=%fused_computation.1.clone.clone.1 | custom fusion | bytes 16793600 | tf_op jit(solution)/shard_map/while/body/eval_jaxpr/jit(_take)/gather | solution.py:40
  196.7 9.2 %fusion.28 = bf16[512,4096]{0,1:T(8,128)(2,1)} fusion(f32[4096,512]{1,0:T(8,128)} %gather_fusion, f32[4096,512]{1,0:T(8,128)} %gather_fusion.1, pred[4096]{0:T(1024)(128)(4,1)S(1)} %get-tuple-element.171, pred[4096]{0:T(1024)(128)(4,1)S(1)} %get-tuple-element.172), kind=kLoop, calls=%fused_computation.4.clone.1 | loop fusion | flops 8388608 | bytes 20979712 | tf_op jit(solution)/shard_map/while/body/eval_jaxpr/convert_element_type | solution.py:41
  205.9 3.4 gather_fusion.2
  209.4 3.7 convolution_add_fusion.4
  213.1 0.2 convolution_add_fusion.5
  213.3 0.0 copy-start
  213.3 0.0 copy-start.1
  213.4 1.0 copy-done
  214.3 0.0 copy-done.1
  214.4 0.0 all-reduce.5.cloned.1.call-update
  214.4 0.0 all-gather.3.cloned.1.call-start
  214.4 77.7 %all-reduce.5.cloned.1.call-done = (f32[64,256]{1,0:T(8,128)}, f32[64,4096]{1,0:T(8,128)}) async-done(((f32[64,256]{1,0:T(8,128)}, f32[64,4096]{1,0:T(8,128)}), (f32[64,256]{1,0:T(8,128)}, f32[64,4096]{1,0:T(8,128)})) %all-reduce.5.cloned.1.call-update) | async-done | bytes 1114128 | tf_op jit(solution)/shard_map/psum | solution.py:59
  292.2 0.0 copy-done.4
  292.2 1.3 multiply_multiply_fusion
  293.5 0.0 copy-start.2
  293.5 0.0 all-gather.3.cloned.1.call-update
  293.5 0.0 all-gather.5.cloned.1.call-start
  293.5 124.9 %all-gather.3.cloned.1.call-done = f32[4096,256]{1,0:T(8,128)} async-done(((f32[8,256]{1,0:T(8,128)}), f32[4096,256]{1,0:T(8,128)}) %all-gather.3.cloned.1.call-update) | async-done | bytes 4194320 | tf_op jit(solution)/shard_map/all_gather | solution.py:77
  418.5 3.9 multiply_reduce_fusion.2
  422.4 96.1 %all-reduce.1 = (f32[256]{0:T(256)S(1)}, f32[256]{0:T(256)S(1)}) all-reduce(f32[256]{0:T(256)S(1)} %get-tuple-element.84, f32[256]{0:T(256)S(1)} %get-tuple-element.83), channel_id=1, replica_groups=mesh['snap'=8,'tile'=64] {'snap','tile'}, use_global_device_ids=true, to_apply=%region_4.6 | all-reduce | flops 512 | bytes 4096 | tf_op jit(solution)/shard_map/psum | solution.py:68
  518.5 0.0 copy-done.2
  518.6 93.8 %psum.46 = f32[256]{0:T(256)S(1)} all-reduce(f32[256]{0:T(256)S(1)} %multiply_reduce_fusion.1), channel_id=1, replica_groups=mesh['snap'=8,'tile'=64] {'snap','tile'}, use_global_device_ids=true, to_apply=%region_9.11 | all-reduce | flops 256 | bytes 2048 | tf_op jit(solution)/shard_map/psum | solution.py:68
  612.4 0.6 multiply_add_fusion.1
  613.0 0.0 copy-start.3
  613.0 0.0 all-gather.5.cloned.1.call-update
  613.0 114.6 %all-gather.5.cloned.1.call-done = f32[4096,256]{1,0:T(8,128)} async-done(((f32[8,256]{1,0:T(8,128)}), f32[4096,256]{1,0:T(8,128)}) %all-gather.5.cloned.1.call-update) | async-done | bytes 4194320 | tf_op jit(solution)/shard_map/all_gather | solution.py:77
  727.6 3.9 multiply_reduce_fusion
  731.5 96.2 %psum.47 = f32[256]{0:T(256)S(1)} all-reduce(f32[256]{0:T(256)S(1)} %get-tuple-element.114), channel_id=1, replica_groups=mesh['snap'=8,'tile'=64] {'snap','tile'}, use_global_device_ids=true, to_apply=%region_11.13 | all-reduce | flops 256 | bytes 2048 | tf_op jit(solution)/shard_map/psum | solution.py:82
  827.7 0.0 copy-done.3
  827.7 0.6 multiply_subtract_fusion
  (19 shorter events, 0.2 us)
Async XLA Ops:
  7.2 285.0 %all-reduce.5.cloned.1.call-start = ((), (), s32[]{:S(2)}) async-start(), calls=%async_computation.2 | async-start | bytes 2228224 | tf_op jit(solution)/shard_map/psum | solution.py:59
  112.0 180.1 %copy-start.4 = (s32[8,256]{1,0:T(8,128)S(1)}, s32[8,256]{1,0:T(8,128)}, u32[]{:S(2)}) copy-start(s32[8,256]{1,0:T(8,128)} %param.11) | copy-start | bytes 24580
  213.3 1.0 copy-start
  213.3 1.0 copy-start.1
  214.4 204.1 %all-gather.3.cloned.1.call-start = ((), (), s32[]{:S(2)}) async-start(), calls=%async_computation | async-start | bytes 4202496 | tf_op jit(solution)/shard_map/all_gather | solution.py:77
  293.5 225.1 %copy-start.2 = (f32[8,256]{1,0:T(8,128)S(1)}, f32[8,256]{1,0:T(8,128)}, u32[]{:S(2)}) copy-start(f32[8,256]{1,0:T(8,128)} %multiply_multiply_fusion) | copy-start | bytes 24580
  293.5 434.1 %all-gather.5.cloned.1.call-start = ((), (), s32[]{:S(2)}) async-start(), calls=%async_computation.1 | async-start | bytes 4202496 | tf_op jit(solution)/shard_map/all_gather | solution.py:77
  613.0 214.7 %copy-start.3 = (f32[8,256]{1,0:T(8,128)S(1)}, f32[8,256]{1,0:T(8,128)}, u32[]{:S(2)}) copy-start(f32[8,256]{1,0:T(8,128)} %multiply_add_fusion.1) | copy-start | bytes 24580
Sparse Core Ops, SparseCore 0:
  214.5 77.6 all-reduce.4
  297.6 120.7 all-gather.2
  613.1 114.4 all-gather.4
where the time goes:
time: 835 us
  blocking collectives  390 us (47%)
  waiting for transfers between devices  317 us (38%)
  local copies, waits for them, and re-layouts  76.7 us (9%)
  other arithmetic  21.2 us (3%)
  matrix products  15.7 us (2%)
  between operations  13.8 us (2%)
    all_gather x2, waiting for transfers between devices, body(): lax.all_gather(direction, ('snap', 'tile'), axis=0, tiled=True)  239 us
    psum x2, blocking collectives, energy_of(): return lax.psum(jnp.sum(vector * vector, axis=0), ('snap', 'tile'))  190 us
    psum x1, blocking collectives, body(): lax.psum(jnp.sum(direction * image, axis=0), ('snap', 'tile'))  96.2 us
    psum x1, waiting for transfers between devices, body(): gram_all, cross_all = lax.psum((gram_part, cross_part), 'snap')  77.7 us
    all_gather x1, blocking collectives, body(): rows_in = lax.all_gather(modes, 'tile', axis=0, tiled=True)  54.4 us
    all_gather x1, blocking collectives, body(): lax.all_gather(targets, 'tile', axis=0, tiled=True)  49.5 us
    gather x2, local copies, waits for them, and re-layouts, inner(): jnp.take(extended, first_factor, axis=1)  33.8 us
    gather x2, local copies, waits for them, and re-layouts, inner(): jnp.take(extended, second_factor, axis=1)  33.7 us
  transfers between devices with their start and end apart: 3, of which 3 were waited for; matrix products, arithmetic and copies ran while one was open for 0% of the time, Pallas kernels for 0%

commit v1 on v0

--- a/solution.py
+++ b/solution.py
@@ -79,7 +79,15 @@
             preferred_element_type=jnp.float32,
         )
         image = support_mask * product
-        step_len = energy / lax.psum(jnp.sum(direction * image, axis=0), ("snap", "tile"))
+
+        def _answer_unit(inner_x):
+            net_axis = "snap"
+            mesh_name = "tile"
+            for i0 in (mesh_name, net_axis):
+                inner_x = lax.psum(inner_x, i0)
+            return inner_x
+
+        step_len = energy / _answer_unit(jnp.sum(direction * image, axis=0))
         coeffs = coeffs + step_len * direction
         resid = resid - step_len * image
         if step + 1 < ITERS:

time: 835 us -> 1020 us (1.22)
  blocking collectives: 390 us -> 571 us
    psum x1 -> x4, blocking collectives: 96.2 us -> 273 us  [_answer_unit(): inner_x = lax.psum(inner_x, i0)]
where the time goes in v1:
time: 1020 us; the launch traced here: 1010 us
  blocking collectives  571 us (56%)
  waiting for transfers between devices  315 us (31%)
  local copies, waits for them, and re-layouts  76.3 us (7%)
  other arithmetic  21.2 us (2%)
  matrix products  15.7 us (2%)
  between operations  13.8 us (1%)
    psum x4, blocking collectives, _answer_unit(): inner_x = lax.psum(inner_x, i0)  273 us
    all_gather x2, waiting for transfers between devices, body(): lax.all_gather(direction, ('snap', 'tile'), axis=0, tiled=True)  237 us
    psum x2, blocking collectives, energy_of(): return lax.psum(jnp.sum(vector * vector, axis=0), ('snap', 'tile'))  195 us
    psum x1, waiting for transfers between devices, body(): gram_all, cross_all = lax.psum((gram_part, cross_part), 'snap')  77.7 us
    all_gather x1, blocking collectives, body(): rows_in = lax.all_gather(modes, 'tile', axis=0, tiled=True)  54.4 us
    all_gather x1, blocking collectives, body(): lax.all_gather(targets, 'tile', axis=0, tiled=True)  49.5 us
    gather x2, local copies, waits for them, and re-layouts, inner(): jnp.take(extended, first_factor, axis=1)  33.6 us
    gather x2, local copies, waits for them, and re-layouts, inner(): jnp.take(extended, second_factor, axis=1)  33.6 us
  transfers between devices with their start and end apart: 3, of which 3 were waited for; matrix products, arithmetic and copies ran while one was open for 0% of the time, Pallas kernels for 0%

profile of v1, /device:TPU:1, one launch (start us, length us, event | category | flops | bytes accessed | tf_op | source)
XLA Modules:
  0.0 1013.8 jit_solution(16876073575547507727)
XLA Ops:
  7.2 0.0 all-reduce.4.cloned.1.call-start
  7.2 0.1 reshape.63
  7.3 0.9 fusion.16
  8.2 54.4 %all_gather.12 = bf16[1024,256]{1,0:T(8,128)(2,1)S(1)} all-gather(bf16[16,256]{1,0:T(8,128)(2,1)} %param.8), channel_id=1, replica_groups=mesh['snap'=8,'tile'=64] {'tile'}, dimensions={0}, use_global_device_ids=true | all-gather | bytes 532480 | tf_op jit(solution)/shard_map/all_gather | solution.py:32
  62.6 49.5 %all_gather.13 = bf16[1024,256]{1,0:T(8,128)(2,1)S(1)} all-gather(bf16[16,256]{1,0:T(8,128)(2,1)} %param.9), channel_id=1, replica_groups=mesh['snap'=8,'tile'=64] {'tile'}, dimensions={0}, use_global_device_ids=true | all-gather | bytes 532480 | tf_op jit(solution)/shard_map/all_gather | solution.py:53
  112.0 0.0 copy-start.4
  112.0 101.0 %while.13 = (s32[]{:T(128)}, f32[64,4096]{1,0:T(8,128)S(1)}, f32[64,256]{1,0:T(8,128)S(1)}, s32[64]{0:T(128)S(1)}, bf16[2,512,256]{2,1,0:T(8,128)(2,1)S(1)}, /*i...) while((s32[]{:T(128)}, f32[64,4096]{1,0:T(8,128)S(1)}, ...), condition=%wide.region_1.3_spmd.clone, body=%wide.region_0.2_spmd.clone.sunk | while | flops 294438976 | bytes 63463412 | solution.py:57
  112.1 0.1 copy.9
  112.2 0.1 pad_convert_fusion.2
  112.3 16.8 %gather_fusion.1 = f32[4096,512]{1,0:T(8,128)} fusion(f32[512,257]{0,1:T(8,128)S(1)} %pad_convert_fusion.2, s32[4096]{0:T(1024)S(1)} %get-tuple-element.168), kind=kCustom, calls=%fused_computation.clone.clone.1 | custom fusion | bytes 16793600 | tf_op jit(solution)/shard_map/while/body/eval_jaxpr/jit(_take)/gather | solution.py:40
  129.1 16.8 %gather_fusion = f32[4096,512]{1,0:T(8,128)} fusion(f32[512,257]{0,1:T(8,128)S(1)} %pad_convert_fusion.2, s32[4096]{0:T(1024)S(1)} %get-tuple-element.167), kind=kCustom, calls=%fused_computation.1.clone.clone.1 | custom fusion | bytes 16793600 | tf_op jit(solution)/shard_map/while/body/eval_jaxpr/jit(_take)/gather | solution.py:40
  145.9 9.2 fusion.28
  155.1 3.4 gather_fusion.2
  158.6 3.7 convolution_add_fusion.4
  162.3 0.2 convolution_add_fusion.5
  162.6 0.1 copy.9
  162.7 0.1 pad_convert_fusion.2
  162.8 16.8 %gather_fusion.1 = f32[4096,512]{1,0:T(8,128)} fusion(f32[512,257]{0,1:T(8,128)S(1)} %pad_convert_fusion.2, s32[4096]{0:T(1024)S(1)} %get-tuple-element.168), kind=kCustom, calls=%fused_computation.clone.clone.1 | custom fusion | bytes 16793600 | tf_op jit(solution)/shard_map/while/body/eval_jaxpr/jit(_take)/gather | solution.py:40
  179.6 16.8 %gather_fusion = f32[4096,512]{1,0:T(8,128)} fusion(f32[512,257]{0,1:T(8,128)S(1)} %pad_convert_fusion.2, s32[4096]{0:T(1024)S(1)} %get-tuple-element.167), kind=kCustom, calls=%fused_computation.1.clone.clone.1 | custom fusion | bytes 16793600 | tf_op jit(solution)/shard_map/while/body/eval_jaxpr/jit(_take)/gather | solution.py:40
  196.4 9.2 fusion.28
  205.6 3.4 gather_fusion.2
  209.1 3.7 convolution_add_fusion.4
  212.8 0.2 convolution_add_fusion.5
  213.0 0.0 copy-start
  213.0 0.0 copy-start.1
  213.0 1.0 copy-done
  214.0 0.0 copy-done.1
  214.0 0.0 all-reduce.4.cloned.1.call-update
  214.1 0.0 all-gather.3.cloned.1.call-start
  214.1 77.7 %all-reduce.4.cloned.1.call-done = (f32[64,256]{1,0:T(8,128)}, f32[64,4096]{1,0:T(8,128)}) async-done(((f32[64,256]{1,0:T(8,128)}, f32[64,4096]{1,0:T(8,128)}), (f32[64,256]{1,0:T(8,128)}, f32[64,4096]{1,0:T(8,128)})) %all-reduce.4.cloned.1.call-update) | async-done | bytes 1114128 | tf_op jit(solution)/shard_map/psum | solution.py:59
  291.8 0.0 copy-done.4
  291.8 1.3 multiply_multiply_fusion
  293.1 0.0 copy-start.2
  293.1 0.0 all-gather.3.cloned.1.call-update
  293.2 0.0 all-gather.5.cloned.1.call-start
  293.2 124.9 %all-gather.3.cloned.1.call-done = f32[4096,256]{1,0:T(8,128)} async-done(((f32[8,256]{1,0:T(8,128)}), f32[4096,256]{1,0:T(8,128)}) %all-gather.3.cloned.1.call-update) | async-done | bytes 4194320 | tf_op jit(solution)/shard_map/all_gather | solution.py:77
  418.1 3.9 multiply_reduce_fusion.2
  422.1 123.7 %psum.59 = f32[256]{0:T(256)S(1)} all-reduce(f32[256]{0:T(256)S(1)} %get-tuple-element.83), channel_id=1, replica_groups=mesh['snap'=8,'tile'=64] {'tile'}, use_global_device_ids=true, to_apply=%region_7.9 | all-reduce | flops 256 | bytes 2048 | tf_op jit(solution)/shard_map/psum | solution.py:87
  545.7 12.7 %psum.60 = f32[256]{0:T(256)S(1)} all-reduce(f32[256]{0:T(256)S(1)} %psum.59), channel_id=1, replica_groups=mesh['snap'=8,'tile'=64] {'snap'}, use_global_device_ids=true, to_apply=%region_8.10 | all-reduce | flops 256 | bytes 2048 | tf_op jit(solution)/shard_map/psum | solution.py:87
  558.4 99.0 %psum.57 = f32[256]{0:T(256)S(1)} all-reduce(f32[256]{0:T(256)S(1)} %get-tuple-element.84), channel_id=1, replica_groups=mesh['snap'=8,'tile'=64] {'snap','tile'}, use_global_device_ids=true, to_apply=%region_4.6 | all-reduce | flops 256 | bytes 2048 | tf_op jit(solution)/shard_map/psum | solution.py:68
  657.4 0.0 copy-done.2
  657.5 95.7 %psum.61 = f32[256]{0:T(256)S(1)} all-reduce(f32[256]{0:T(256)S(1)} %multiply_reduce_fusion.1), channel_id=1, replica_groups=mesh['snap'=8,'tile'=64] {'snap','tile'}, use_global_device_ids=true, to_apply=%region_10.12 | all-reduce | flops 256 | bytes 2048 | tf_op jit(solution)/shard_map/psum | solution.py:68
  753.2 0.6 multiply_add_fusion.1
  753.8 0.0 copy-start.3
  753.8 0.0 all-gather.5.cloned.1.call-update
  753.8 112.5 %all-gather.5.cloned.1.call-done = f32[4096,256]{1,0:T(8,128)} async-done(((f32[8,256]{1,0:T(8,128)}), f32[4096,256]{1,0:T(8,128)}) %all-gather.5.cloned.1.call-update) | async-done | bytes 4194320 | tf_op jit(solution)/shard_map/all_gather | solution.py:77
  866.3 3.9 multiply_reduce_fusion
  870.3 123.7 %psum.62 = f32[256]{0:T(256)S(1)} all-reduce(f32[256]{0:T(256)S(1)} %get-tuple-element.112), channel_id=1, replica_groups=mesh['snap'=8,'tile'=64] {'tile'}, use_global_device_ids=true, to_apply=%region_12.14 | all-reduce | flops 256 | bytes 2048 | tf_op jit(solution)/shard_map/psum | solution.py:87
  993.9 12.7 %psum.63 = f32[256]{0:T(256)S(1)} all-reduce(f32[256]{0:T(256)S(1)} %psum.62), channel_id=1, replica_groups=mesh['snap'=8,'tile'=64] {'snap'}, use_global_device_ids=true, to_apply=%region_13.15 | all-reduce | flops 256 | bytes 2048 | tf_op jit(solution)/shard_map/psum | solution.py:87
  1006.6 0.0 copy-done.3
  1006.6 0.6 multiply_subtract_fusion
  (19 shorter events, 0.2 us)
Async XLA Ops:
  7.2 284.7 %all-reduce.4.cloned.1.call-start = ((), (), s32[]{:S(2)}) async-start(), calls=%async_computation.2 | async-start | bytes 2228224 | tf_op jit(solution)/shard_map/psum | solution.py:59
  112.0 179.8 %copy-start.4 = (s32[8,256]{1,0:T(8,128)S(1)}, s32[8,256]{1,0:T(8,128)}, u32[]{:S(2)}) copy-start(s32[8,256]{1,0:T(8,128)} %param.11) | copy-start | bytes 24580
  213.0 1.0 copy-start
  213.0 1.0 copy-start.1
  214.1 204.1 %all-gather.3.cloned.1.call-start = ((), (), s32[]{:S(2)}) async-start(), calls=%async_computation | async-start | bytes 4202496 | tf_op jit(solution)/shard_map/all_gather | solution.py:77
  293.1 364.3 %copy-start.2 = (f32[8,256]{1,0:T(8,128)S(1)}, f32[8,256]{1,0:T(8,128)}, u32[]{:S(2)}) copy-start(f32[8,256]{1,0:T(8,128)} %multiply_multiply_fusion) | copy-start | bytes 24580
  293.2 573.2 %all-gather.5.cloned.1.call-start = ((), (), s32[]{:S(2)}) async-start(), calls=%async_computation.1 | async-start | bytes 4202496 | tf_op jit(solution)/shard_map/all_gather | solution.py:77
  753.8 252.8 %copy-start.3 = (f32[8,256]{1,0:T(8,128)S(1)}, f32[8,256]{1,0:T(8,128)}, u32[]{:S(2)}) copy-start(f32[8,256]{1,0:T(8,128)} %multiply_add_fusion.1) | copy-start | bytes 24580
Sparse Core Ops, SparseCore 0:
  214.2 77.6 all-reduce.3
  297.3 120.7 all-gather.2
  753.9 112.3 all-gather.4
